TPU v7x, 256 devices: a whole 4x4x8 slice. The times are simulated.
256 devices in a mesh: seq: 64 (over z, x_hi, y), head: 4 (over x_lo, core).
Axes of the slice: x: 4 (x_hi: 2, x_lo: 2; x = x_hi * 2 + x_lo), y: 4, z: 8, core: 2. Of those that a mesh axis runs over, the one named last changes fastest.
Arguments:
- hidden_in: bfloat16 [5120, 7168], P('seq', 'head'), may hold values from -6 to 6
- w_down: bfloat16 [7168, 576], P('head'), may hold values from -0.0625 to 0.0625
- kv_gain: bfloat16 [512], replicated, may hold values from 0.099609375 to 1.8984375
- queries: bfloat16 [5120, 12288], P('seq', 'head'), may hold values from -140 to 140
- w_key: bfloat16 [512, 8192], P(None, 'head'), may hold values from -0.25 to 0.25
- w_value: bfloat16 [512, 8192], P(None, 'head'), may hold values from -1.25 to 1.25
Outputs:
- values_out: bfloat16 [5120, 8192], P('seq', 'head')
All inputs are finite; a program needn't handle non-finite values.
Results may differ from a plain program's by a relative error of at most 0.013.
The roundings to bfloat16 on the way count: a program that leaves them out, or rounds other values in their place, can miss the bound.
Values may be sent and summed in bfloat16 or wider, within the bound.
A program may use at most 128 MiB of HBM per device.

v0:
```python
import jax
import jax.numpy as jnp
from jax import lax
from jax.sharding import PartitionSpec as P

ROPE = 64
NOPE = 128
VDIM = 128


def fold_order(indices, per_device, devices):
    half_rows = per_device // 2
    device = indices // per_device
    offset_in = indices % per_device
    early = device * half_rows + offset_in
    late = (2 * devices - 1 - device) * half_rows + offset_in - half_rows
    return jnp.where(offset_in < half_rows, early, late)


def rotate(vectors, positions):
    width = vectors.shape[-1] // 2
    inverse = 10000.0 ** (-jnp.arange(width, dtype=jnp.float32) / width)
    angles = positions.astype(jnp.float32)[..., None] * inverse
    cosine = jnp.cos(angles)
    sine = jnp.sin(angles)
    leading = vectors[..., :width]
    trailing = vectors[..., width:]
    return jnp.concatenate(
        [leading * cosine - trailing * sine, trailing * cosine + leading * sine], -1
    )


def contract_last(left, right):
    return lax.dot_general(
        left, right, (((1,), (1,)), ((), ())), preferred_element_type=jnp.float32
    )


def unchanged(state):
    return state


def on_device(hidden_in, w_down, kv_gain, queries, w_key, w_value):
    seq_count = lax.axis_size("seq")
    seq_index = lax.axis_index("seq")
    tok_rows = queries.shape[0]
    half_rows = tok_rows // 2
    latent_width = w_key.shape[0]
    heads_here = w_key.shape[1] // NOPE
    partial_value = jnp.dot(hidden_in, w_down, preferred_element_type=jnp.float32)
    projected = lax.psum(partial_value, "head")
    first_row = seq_index * tok_rows
    key_positions = fold_order(
        first_row + jnp.arange(projected.shape[0], dtype=jnp.int32), tok_rows, seq_count
    )
    raw_latent = projected[:, :latent_width]
    mean_square = jnp.mean(raw_latent * raw_latent, axis=1, keepdims=True)
    latent = (raw_latent * lax.rsqrt(mean_square + 1e-06) * kv_gain.astype(jnp.float32)).astype(
        jnp.bfloat16
    )
    key_rope = rotate(projected[:, latent_width:], key_positions).astype(jnp.bfloat16)
    query_positions = fold_order(
        seq_index * tok_rows + jnp.arange(tok_rows, dtype=jnp.int32), tok_rows, seq_count
    )
    scale_factor = (NOPE + ROPE) ** (-0.5)
    shaped = queries.reshape(tok_rows, heads_here, NOPE + ROPE)
    query_rope = (
        rotate(shaped[:, :, NOPE:].astype(jnp.float32), query_positions[:, None]) * scale_factor
    ).astype(jnp.bfloat16)
    key_weight = w_key.reshape(latent_width, heads_here, NOPE)
    query_latent = jnp.einsum(
        "thd,chd->thc", shaped[:, :, :NOPE], key_weight, preferred_element_type=jnp.float32
    )
    query_latent = (query_latent * scale_factor).astype(jnp.bfloat16)
    latent_blocks = []
    rope_blocks = []
    row_positions = []
    highest_query = []
    for half_index in range(2):
        lower = half_index * half_rows
        latent_blocks.append(
            query_latent[lower : lower + half_rows].reshape(half_rows * heads_here, latent_width)
        )
        rope_blocks.append(
            query_rope[lower : lower + half_rows].reshape(half_rows * heads_here, ROPE)
        )
        half_positions = query_positions[lower : lower + half_rows]
        row_positions.append(jnp.repeat(half_positions, heads_here))
        highest_query.append(jnp.max(half_positions))
    score_rows = half_rows * heads_here
    start_state = (
        jnp.full((score_rows,), -1e30, jnp.float32),
        jnp.zeros((score_rows,), jnp.float32),
        jnp.zeros((score_rows, latent_width), jnp.float32),
    )
    carry = (start_state, start_state)
    latent_piece = lax.all_gather(latent, "seq", axis=0, tiled=True)
    rope_piece = lax.all_gather(key_rope, "seq", axis=0, tiled=True)
    piece_positions = fold_order(
        jnp.arange(latent_piece.shape[0], dtype=jnp.int32), tok_rows, seq_count
    )
    lowest_key = jnp.min(piece_positions)
    updated = []
    for absorb_half_index in range(2):

        def attend(state):
            running_top, running_total, running_sum = state
            scores = contract_last(latent_blocks[absorb_half_index], latent_piece)
            scores = scores + contract_last(rope_blocks[absorb_half_index], rope_piece)
            allowed = piece_positions[None, :] <= row_positions[absorb_half_index][:, None]
            scores = jnp.where(allowed, scores, -1e30)
            new_top = jnp.maximum(running_top, jnp.max(scores, axis=1))
            weights = jnp.where(allowed, jnp.exp(scores - new_top[:, None]), 0.0)
            new_total = jnp.sum(weights, axis=1)
            product = jnp.dot(
                weights.astype(jnp.bfloat16), latent_piece, preferred_element_type=jnp.float32
            )
            return (new_top, new_total, product)

        updated.append(
            lax.cond(
                lowest_key > highest_query[absorb_half_index],
                unchanged,
                attend,
                carry[absorb_half_index],
            )
        )
    states = tuple(updated)
    finished = []
    for half_index in range(2):
        running_top, running_total, running_sum = states[half_index]
        attended = (running_sum / running_total[:, None]).astype(jnp.bfloat16)
        finished.append(attended.reshape(half_rows, heads_here, latent_width))
    attended = jnp.concatenate(finished, 0)
    value_weight = w_value.reshape(latent_width, heads_here, VDIM)
    values = jnp.einsum("thc,chd->thd", attended, value_weight, preferred_element_type=jnp.float32)
    return values.reshape(tok_rows, heads_here * VDIM).astype(jnp.bfloat16)


def solution(mesh):
    in_specs = (
        P("seq", "head"),
        P("head", None),
        P(),
        P("seq", "head"),
        P(None, "head"),
        P(None, "head"),
    )
    out_specs = P("seq", "head")
    return jax.shard_map(
        on_device, mesh=mesh, in_specs=in_specs, out_specs=out_specs, check_vma=False
    )
```

profile of v0, /device:TPU:2, one launch (start us, length us, event | category | flops | bytes accessed | tf_op | source)
XLA Modules:
  0.0 320.3 jit_solution(15941549153875839825)
XLA Ops:
  6.5 0.0 copy-start
  6.5 0.0 all-reduce.2.cloned.1.call-start
  6.5 3.2 %fusion.63 = f32[80,576]{1,0:T(8,128)} fusion(bf16[80,1792]{1,0:T(8,128)(2,1)} %param.10, bf16[1792,576]{0,1:T(8,128)(2,1)} %param.11), kind=kOutput, calls=%fused_computation.81 | convolution fusion | flops 165150720 | bytes 2535424 | tf_op jit(solution)/shard_map/dot_general | solution.py:50
  9.8 0.0 all-reduce.2.cloned.1.call-update
  9.8 0.0 all-gather.3.cloned.1.call-start
  9.9 0.7 convert_element_type.63
  10.5 42.1 %all-reduce.2.cloned.1.call-done = f32[80,576]{1,0:T(8,128)} async-done(((f32[80,576]{1,0:T(8,128)}), f32[80,576]{1,0:T(8,128)}) %all-reduce.2.cloned.1.call-update) | async-done | bytes 184336 | tf_op jit(solution)/shard_map/psum | solution.py:51
  52.6 1.0 multiply_reduce_fusion
  53.6 1.6 multiply_convert_fusion.1
  55.3 0.0 all-gather.3.cloned.1.call-update
  55.3 0.6 fusion.56
  56.0 0.8 slice_reduce_fusion.1
  59.1 1.8 reshape.177
  60.9 0.1 slice.57
  61.1 0.9 slice_convert_fusion
  62.0 0.0 copy-done
  62.0 1.9 fusion.26
  63.9 0.0 copy-start.2
  63.9 0.0 copy-start.3
  63.9 1.2 subtract_convert_fusion
  65.1 0.1 maximum_bitcast_fusion
  65.2 0.1 copy.32
  65.3 188.3 %all-gather = bf16[64,80,64]{1,2,0:T(8,128)(2,1)S(1)} all-gather(bf16[1,80,64]{1,2,0:T(8,128)(2,1)S(1)} %copy.32), channel_id=1, replica_groups=mesh['seq'=64,'head'=4] {'seq'}, dimensions={0}, use_global_device_ids=true | all-gather | bytes 665600 | tf_op jit(solution)/shard_map/all_gather | solution.py:98
  253.6 1.7 copy.33
  255.2 2.6 reshape.182
  257.8 0.0 copy-done.2
  257.8 0.2 multiply_subtract_fusion
  258.1 0.2 fusion.42
  258.3 0.0 all-gather.3.cloned.1.call-done
  258.4 0.0 copy-done.3
  258.4 24.1 %conditional.2 = (f32[640]{0:T(1024)S(1)}, f32[640,512]{1,0:T(8,128)}) conditional(s32[]{:T(128)} %convert_element_type.60, (s32[5120]{0:T(1024)S(1)}, s32[40]{0:T(128)S(1)}, bf16[80,16,512]{2,0,1:T(8,128)(2,1)S(1)}, bf16[5120,512]{1,0:T(8,128)(2,1)}, bf16[80,16,64]{2,1,0:T(8,128)(2,1)S(1)}, /*index=5*/bf16[5120,64]{0,1:T(8,128)(2,1)S(1)}) %tuple.50, ...), branch_computations={%region_4.7_spmd, %region_7.8_spmd} | conditional | flops 7169637888 | bytes 98642144 | solution.py:121
  258.6 0.1 broadcast_in_dim.27
  258.6 0.1 le.16
  258.7 0.7 copy.34
  259.5 0.0 slice-start
  259.5 9.2 %fusion.61 = f32[640,5120]{1,0:T(8,128)} fusion(bf16[640,512]{1,0:T(8,128)(2,1)S(1)} %bitcast.56, bf16[5120,512]{1,0:T(8,128)(2,1)} %get-tuple-element.42), kind=kOutput, calls=%fused_computation.79 | convolution fusion | flops 3355443200 | bytes 19005440 | tf_op jit(solution)/shard_map/cond/branch_0_fun/dot_general | solution.py:34
  268.7 0.0 slice-start.1
  268.7 6.1 %fusion.59 = (f32[640]{0:T(1024)S(1)}, f32[640,5120]{1,0:T(8,128)S(1)}) fusion(f32[640,5120]{1,0:T(8,128)} %fusion.61, bf16[640,64]{1,0:T(8,128)(2,1)S(1)} %bitcast.60, bf16[5120,64]{0,1:T(8,128)(2,1)S(1)} %get-tuple-element.100, s32[640]{0:T(1024)S(1)} %le.16, s32[5120]{0:T(1024)S(1)} %get-tuple-element.39), kind=kOutput, calls=%fused_computation.77 | convolution fusion | flops 432536960 | bytes 26977280 | tf_op jit(solution)/shard_map/cond/branch_0_fun/dot_general | solution.py:34
  274.9 0.0 slice-done
  274.9 0.0 slice-done.1
  274.9 4.9 %fusion.2 = f32[640,512]{1,0:T(8,128)} fusion(bf16[5120,512]{1,0:T(8,128)(2,1)S(1)} %bitcast.53, f32[640,5120]{1,0:T(8,128)S(1)} %get-tuple-element.110, f32[640]{0:T(1024)S(1)} %broadcast_maximum_fusion, s32[5120]{0:T(1024)S(1)} %get-tuple-element.39, s32[640]{0:T(1024)S(1)} %le.16), kind=kOutput, calls=%fused_computation.4 | convolution fusion | flops 3368550400 | bytes 19686400 | tf_op jit(solution)/shard_map/cond/branch_0_fun/dot_general | solution.py:115
  279.7 2.7 fusion.1
  282.4 1.5 divide_convert_fusion.1
  283.9 0.4 copy.38
  284.3 24.1 %conditional.3 = (f32[640]{0:T(1024)S(1)}, f32[640,512]{1,0:T(8,128)}) conditional(s32[]{:T(128)} %convert_element_type.69, (s32[5120]{0:T(1024)S(1)}, s32[40]{0:T(128)S(1)}, bf16[80,16,512]{2,0,1:T(8,128)(2,1)S(1)}, bf16[5120,512]{1,0:T(8,128)(2,1)}, bf16[80,16,64]{2,1,0:T(8,128)(2,1)S(1)}, /*index=5*/bf16[5120,64]{0,1:T(8,128)(2,1)S(1)}) %tuple.51, ...), branch_computations={%region_9.12_spmd, %region_12.13_spmd} | conditional | flops 7169637888 | bytes 98642144 | solution.py:121
  284.5 0.1 broadcast_in_dim.46
  284.6 0.1 le.20
  284.7 0.7 copy.36
  285.5 0.0 slice-start.2
  285.5 9.2 %fusion.62 = f32[640,5120]{1,0:T(8,128)} fusion(bf16[640,512]{1,0:T(8,128)(2,1)S(1)} %bitcast.57, bf16[5120,512]{1,0:T(8,128)(2,1)} %get-tuple-element.48), kind=kOutput, calls=%fused_computation.80 | convolution fusion | flops 3355443200 | bytes 19005440 | tf_op jit(solution)/shard_map/cond/branch_0_fun/dot_general | solution.py:34
  294.7 0.0 slice-start.3
  294.7 6.1 %fusion.60 = (f32[640]{0:T(1024)S(1)}, f32[640,5120]{1,0:T(8,128)S(1)}) fusion(f32[640,5120]{1,0:T(8,128)} %fusion.62, bf16[640,64]{1,0:T(8,128)(2,1)S(1)} %bitcast.61, bf16[5120,64]{0,1:T(8,128)(2,1)S(1)} %get-tuple-element.106, s32[640]{0:T(1024)S(1)} %le.20, s32[5120]{0:T(1024)S(1)} %get-tuple-element.45), kind=kOutput, calls=%fused_computation.78 | convolution fusion | flops 432536960 | bytes 26977280 | tf_op jit(solution)/shard_map/cond/branch_0_fun/dot_general | solution.py:34
  300.8 0.0 slice-done.2
  300.8 0.0 slice-done.3
  300.8 4.9 %fusion.11 = f32[640,512]{1,0:T(8,128)} fusion(bf16[5120,512]{1,0:T(8,128)(2,1)S(1)} %bitcast.55, f32[640,5120]{1,0:T(8,128)S(1)} %get-tuple-element.112, f32[640]{0:T(1024)S(1)} %broadcast_maximum_fusion.1, s32[5120]{0:T(1024)S(1)} %get-tuple-element.45, s32[640]{0:T(1024)S(1)} %le.20), kind=kOutput, calls=%fused_computation.15 | convolution fusion | flops 3368550400 | bytes 19686400 | tf_op jit(solution)/shard_map/cond/branch_0_fun/dot_general | solution.py:115
  305.7 2.7 fusion.10
  308.4 0.0 copy-start.1
  308.4 1.6 divide_convert_fusion
  310.0 0.4 copy.39
  310.4 2.2 fusion.37
  312.6 0.8 copy.67
  313.4 0.0 copy-done.1
  (13 shorter events, 0.2 us)
Async XLA Ops:
  6.5 55.4 %copy-start = (bf16[512,2048]{1,0:T(8,128)(2,1)S(1)}, bf16[512,2048]{1,0:T(8,128)(2,1)}, u32[]{:S(2)}) copy-start(bf16[512,2048]{1,0:T(8,128)(2,1)} %param.14) | copy-start | bytes 6291460
  6.5 46.1 %all-reduce.2.cloned.1.call-start = ((), (), s32[]{:S(2)}) async-start(), calls=%async_computation | async-start | bytes 409600 | tf_op jit(solution)/shard_map/psum | solution.py:51
  9.8 248.6 %all-gather.3.cloned.1.call-start = ((), (), s32[]{:S(2)}) async-start(), calls=%async_computation.1 | async-start | bytes 5324800 | tf_op jit(solution)/shard_map/all_gather | solution.py:97
  63.9 193.9 %copy-start.2 = (f32[80,16,64]{2,1,0:T(8,128)S(1)}, f32[80,16,64]{2,1,0:T(8,128)}, u32[]{:S(2)}) copy-start(f32[80,16,64]{2,1,0:T(8,128)} %slice_convert_fusion) | copy-start | bytes 983044
  63.9 194.5 %copy-start.3 = (bf16[80,16,512]{2,0,1:T(8,128)(2,1)S(1)}, bf16[80,16,512]{2,0,1:T(8,128)(2,1)}, u32[]{:S(2)}) copy-start(bf16[80,16,512]{2,0,1:T(8,128)(2,1)} %fusion.26) | copy-start | bytes 3932164
  259.5 15.3 %slice-start = ((s8[5242880]{0:T(1024)(128)(4,1)}), s8[1048576]{0:T(1024)(128)(4,1)S(1)}, s32[]{:S(2)}) async-start(s8[5242880]{0:T(1024)(128)(4,1)} %bitcast.52), calls=%async_computation.2 | async-start | bytes 2097152 | tf_op jit(solution)/shard_map/cond
  268.7 6.2 %slice-start.1 = ((s8[5242880]{0:T(1024)(128)(4,1)}), s8[4194304]{0:T(1024)(128)(4,1)S(1)}, s32[]{:S(2)}) async-start(s8[5242880]{0:T(1024)(128)(4,1)} %bitcast.52), calls=%async_computation.3 | async-start | bytes 8388608 | tf_op jit(solution)/shard_map/cond
  285.5 15.3 %slice-start.2 = ((s8[5242880]{0:T(1024)(128)(4,1)}), s8[1048576]{0:T(1024)(128)(4,1)S(1)}, s32[]{:S(2)}) async-start(s8[5242880]{0:T(1024)(128)(4,1)} %bitcast.54), calls=%async_computation.4 | async-start | bytes 2097152 | tf_op jit(solution)/shard_map/cond
  294.7 6.2 %slice-start.3 = ((s8[5242880]{0:T(1024)(128)(4,1)}), s8[4194304]{0:T(1024)(128)(4,1)S(1)}, s32[]{:S(2)}) async-start(s8[5242880]{0:T(1024)(128)(4,1)} %bitcast.54), calls=%async_computation.5 | async-start | bytes 8388608 | tf_op jit(solution)/shard_map/cond
  308.4 5.0 %copy-start.1 = (bf16[512,2048]{1,0:T(8,128)(2,1)S(1)}, bf16[512,2048]{1,0:T(8,128)(2,1)}, u32[]{:S(2)}) copy-start(bf16[512,2048]{1,0:T(8,128)(2,1)} %param.14) | copy-start | bytes 6291460
Sparse Core Ops, SparseCore 0:
  10.0 42.5 all-reduce.1
  56.8 136.5 all-gather.2
where the time goes:
time: 321 us; the launch traced here: 320 us
  blocking collectives  188 us (59%)
  matrix products  47.7 us (15%)
  waiting for transfers between devices  42.1 us (13%)
  other arithmetic  16 us (5%)
  between operations  16 us (5%)
  local copies, waits for them, and re-layouts  9.6 us (3%)
    all_gather x1, blocking collectives, on_device(): rope_piece = lax.all_gather(key_rope, 'seq', axis=0, tiled=True)  188 us
    psum x1, waiting for transfers between devices, on_device(): projected = lax.psum(partial_value, 'head')  42.1 us
    dot_general x4, matrix products, contract_last(): lax.dot_general(left, right, (((1,), (1,)), ((), ())), preferred_element_...  30.6 us
    dot_general x2, matrix products, attend(): jnp.dot(weights.astype(jnp.bfloat16), latent_piece, preferred_element_typ...  9.72 us
  transfers between devices with their start and end apart: 2, of which 1 were waited for; matrix products, arithmetic and copies ran while one was open for 4% of the time, Pallas kernels for 0%

commit v1 on v0

v1 whole, which is shorter than its diff:
```python
import functools

import jax
import jax.numpy as jnp
import numpy as np
from jax import lax
from jax.experimental import pallas as pl
from jax.experimental.pallas import tpu as pltpu
from jax.sharding import PartitionSpec as P

F32 = jnp.float32
BF16 = jnp.bfloat16
MESH = pl.DeviceIdType.MESH
LAT, ROPE, NOPE, VDIM = 512, 64, 128, 128
TOK, HALF, HEADS = 80, 40, 16
ROWS = HALF * HEADS
EARLY = 2560
STEP = 512
NT = (((1,), (1,)), ((), ()))
SCALE = (NOPE + ROPE) ** (-0.5)
N_SEMS = 160


def wrap(value, size):
    return lax.rem(value + 2 * size, size)


def place():
    s = lax.axis_index("seq")
    h = lax.axis_index("head")
    x = lax.rem(lax.div(s, 4), 2) * 2 + lax.div(h, 2)
    return x, lax.rem(s, 4), lax.div(s, 8), lax.rem(h, 2)


def device(x, y, z, c):
    x, y, z = wrap(x, 4), wrap(y, 4), wrap(z, 8)
    return (z * 8 + lax.div(x, 2) * 4 + y, lax.rem(x, 2) * 2 + c)


class Comm:
    def __init__(self, send_sems, recv_sems):
        self.send_sems, self.recv_sems = send_sems, recv_sems
        self.sent, self.names = [], {}

    def copy(self, name, src, dst, to):
        i = self.names.setdefault(name, len(self.names))
        return pltpu.make_async_remote_copy(
            src, dst, self.send_sems.at[i], self.recv_sems.at[i], device_id=to, device_id_type=MESH
        )

    def send(self, name, src, to, dst=None):
        copy = self.copy(name, src, src if dst is None else dst, to)
        copy.start()
        self.sent.append(copy)

    def recv(self, name, ref):
        self.copy(name, ref, ref, device(*place())).wait_recv()

    def drain(self):
        for copy in self.sent:
            copy.wait_send()
        self.sent = []


PLANE = [(dx, dy) for dx in range(4) for dy in range(4) if dx or dy]


def greet():
    x, y, z, c = place()
    bar = pltpu.get_barrier_semaphore()
    for dz in range(1, 8):
        pl.semaphore_signal(bar, 1, device_id=device(x, y, z + dz, c), device_id_type=MESH)
    for dx, dy in PLANE:
        pl.semaphore_signal(bar, 1, device_id=device(x + dx, y + dy, z, c), device_id_type=MESH)
    pl.semaphore_signal(bar, 1, device_id=device(x, y, z, 1 - c), device_id_type=MESH)


def meet():
    pl.semaphore_wait(pltpu.get_barrier_semaphore(), 7 + len(PLANE) + 1)


def gather_first(cm, KA, KB, KC):
    x, y, z, c = place()
    for dz in (4, 3, 5, 2, 6, 1, 7):
        cm.send(f"az{dz}", KA.at[c, y, x, z], device(x, y, z + dz, c))
        cm.send(f"bz{dz}", KB.at[c, x, y, z], device(x, y, z + dz, c))
    order = sorted(PLANE, key=lambda t: -(min(t[0], 4 - t[0]) + min(t[1], 4 - t[1])))
    for dx, dy in order:
        cm.send(f"cp{dx}{dy}", KC.at[c, z, x, y], device(x + dx, y + dy, z, c))


def gather_rest(cm, KA, KB, KC):
    x, y, z, c = place()
    sibling = device(x, y, z, 1 - c)

    def X(d):
        return wrap(x + d, 4)

    def Y(d):
        return wrap(y + d, 4)

    def Z(d):
        return wrap(z + d, 8)

    def share(name, ref):
        cm.send("s" + name, ref, sibling)

    for dz in range(1, 8):
        cm.recv(f"az{dz}", KA.at[c, y, x, Z(-dz)])
    for d in (1, -1):
        cm.send(f"ax{d}", KA.at[c, y, x], device(x + d, y, z, c))
    for d in (1, -1):
        cm.send(f"ay{d}_0", KA.at[c, y, x], device(x, y + d, z, c))
    cm.send("ax2", KA.at[c, y, x], device(x + 2, y, z, c))
    share("a00", KA.at[c, y, x])
    for dz in range(1, 8):
        cm.recv(f"bz{dz}", KB.at[c, x, y, Z(-dz)])
    for d in (1, -1):
        cm.send(f"by{d}", KB.at[c, x, y], device(x, y + d, z, c))
    for d in (1, -1):
        cm.send(f"bx{d}_0", KB.at[c, x, y], device(x + d, y, z, c))
    cm.send("by2", KB.at[c, x, y], device(x, y + 2, z, c))
    share("b00", KB.at[c, x, y])
    for dx, dy in PLANE:
        cm.recv(f"cp{dx}{dy}", KC.at[c, z, X(-dx), Y(-dy)])
    for d in (1, -1):
        cm.send(f"cz{d}_1", KC.at[c, z], device(x, y, z + d, c))
    share("c0", KC.at[c, z])
    for d in (1, -1):
        cm.recv(f"ax{d}", KA.at[c, y, X(-d)])
        for e in (1, -1):
            cm.send(f"ay{e}_{-d}", KA.at[c, y, X(-d)], device(x, y + e, z, c))
        share(f"a0{-d}", KA.at[c, y, X(-d)])
        cm.recv(f"by{d}", KB.at[c, x, Y(-d)])
        for e in (1, -1):
            cm.send(f"bx{e}_{-d}", KB.at[c, x, Y(-d)], device(x + e, y, z, c))
        share(f"b0{-d}", KB.at[c, x, Y(-d)])

    def pass_a(e, col):
        cm.recv(f"ay{e}_{col}", KA.at[c, Y(-e), X(col)])
        if (e == 1) == (col in (0, 1)):
            cm.send(f"af_{col}", KA.at[c, Y(-e), X(col)], device(x, y + e, z, c))

    def pass_b(e, col):
        cm.recv(f"bx{e}_{col}", KB.at[c, X(-e), Y(col)])
        if (e == 1) == (col in (0, 1)):
            cm.send(f"bf_{col}", KB.at[c, X(-e), Y(col)], device(x + e, y, z, c))

    def pass_c(k):
        for d in (1, -1):
            cm.recv(f"cz{d}_{k}", KC.at[c, Z(-d * k)])
            if k < 3:
                cm.send(f"cz{d}_{k + 1}", KC.at[c, Z(-d * k)], device(x, y, z + d, c))
            else:
                part = slice(0, 2) if d == 1 else slice(2, 4)
                cm.send(f"cz{d}_4", KC.at[c, Z(-d * k), part], device(x, y, z + d, c))
            share(f"cs{d}{k}", KC.at[c, Z(-d * k)])

    pass_a(1, 0)
    pass_b(1, 0)
    pass_c(1)
    cm.recv("ax2", KA.at[c, y, X(2)])
    for e in (1, -1):
        cm.send(f"ay{e}_2", KA.at[c, y, X(2)], device(x, y + e, z, c))
    share("a02", KA.at[c, y, X(2)])
    cm.recv("by2", KB.at[c, x, Y(2)])
    for e in (1, -1):
        cm.send(f"bx{e}_2", KB.at[c, x, Y(2)], device(x + e, y, z, c))
    share("b02", KB.at[c, x, Y(2)])
    for e, col in ((1, 1), (-1, -1)):
        pass_a(e, col)
        pass_b(e, col)
    pass_c(2)
    for e, col in ((-1, 2), (-1, 0), (1, -1), (-1, 1), (1, 2)):
        pass_a(e, col)
        pass_b(e, col)
    for d in (1, -1):
        share(f"a{d}", KA.at[c, Y(d)])
        share(f"b{d}", KB.at[c, X(d)])
    pass_c(3)
    for col in (0, 1, -1, 2):
        cm.recv(f"af_{col}", KA.at[c, Y(2), X(col)])
        cm.recv(f"bf_{col}", KB.at[c, X(2), Y(col)])
    share("a2", KA.at[c, Y(2)])
    share("b2", KB.at[c, X(2)])
    cm.recv("cz1_4", KC.at[c, Z(4), 0:2])
    cm.recv("cz-1_4", KC.at[c, Z(4), 2:4])
    share("c4", KC.at[c, Z(4)])
    o = 1 - c
    for d in (0, 1, -1, 2):
        cm.recv(f"sa0{d}", KA.at[o, y, X(d)])
        cm.recv(f"sb0{d}", KB.at[o, x, Y(d)])
    for d in (1, -1, 2):
        cm.recv(f"sa{d}", KA.at[o, Y(d)])
        cm.recv(f"sb{d}", KB.at[o, X(d)])
    cm.recv("sc0", KC.at[o, z])
    for k in (1, 2, 3):
        for d in (1, -1):
            cm.recv(f"scs{d}{k}", KC.at[o, Z(-d * k)])
    cm.recv("sc4", KC.at[o, Z(4)])


def lanes(shape):
    return lax.broadcasted_iota(jnp.int32, shape, 1)


def rotated(v, cos, sin):
    width = v.shape[1]
    first = (lanes(v.shape) & 63) < 32
    other = jnp.where(first, pltpu.roll(v, width - 32, 1), pltpu.roll(v, 32, 1))
    return v * cos + other * sin


def fifth(value):
    return (value * 205) >> 10


def body(
    hidden_hbm, down_hbm, gain_ref, inv_ref, queries_hbm, wkey_hbm, wvalue_hbm, out_ref,
    hidden, down, queries, wkey, wvalue, part, got1, mine, got2, KA, KB, KC,
    keys, q, kpos, qpos, cos, sin, scores, top, total, acc,
    load_sems, send_sems, recv_sems,
):
    x, y, z, c = place()
    seq = lax.axis_index("seq")
    x_lo = lax.rem(x, 2)
    loads = [
        pltpu.make_async_copy(src, dst, load_sems.at[i])
        for i, (src, dst) in enumerate(
            (
                (hidden_hbm, hidden),
                (down_hbm, down),
                (queries_hbm, queries),
                (wkey_hbm, wkey),
                (wvalue_hbm, wvalue),
            )
        )
    ]
    for load in loads:
        load.start()
    greet()
    cm = Comm(send_sems, recv_sems)

    token = lax.broadcasted_iota(jnp.int32, (TOK, 128), 0)
    lane = lanes((TOK, 128))
    early_pos = seq * HALF
    late_pos = (127 - seq) * HALF
    position = jnp.where(token < HALF, early_pos + token, late_pos + token - HALF)
    angle = position.astype(F32) * inv_ref[...]
    cos[...] = jnp.cos(angle)
    sine = jnp.sin(angle)
    sin[...] = jnp.where((lane & 63) < 32, -sine, sine)

    e = lanes((8, EARLY))
    plane = fifth(e >> 6)
    r = e - 320 * plane
    in_tail = r >= 256
    slot = jnp.where(in_tail, (r - 256) >> 3, (r & 127) >> 4)
    owner = plane * 8 + (slot & 1) * 4 + (slot >> 1)
    kpos[:, 0:EARLY] = owner * HALF + jnp.where(in_tail, 32 + (r & 7), (r >> 7) * 16 + (r & 15))
    kpos[:, EARLY:] = (127 - owner) * HALF + jnp.where(
        in_tail, r & 7, 8 + (r >> 7) * 16 + (r & 15)
    )
    row = lax.broadcasted_iota(jnp.int32, (ROWS, 128), 0)
    row = row - HALF * fifth(row >> 3)
    qpos[0:ROWS] = early_pos + row
    qpos[ROWS:] = late_pos + row

    loads[0].wait()
    loads[1].wait()
    partial = jnp.dot(hidden[...], down[...], preferred_element_type=F32)
    part[0] = partial[0:48, 0:LAT]
    part[1, 0:32] = partial[48:80, 0:LAT]
    rope = jnp.concatenate([partial[:, LAT:], jnp.zeros((TOK, 128 - ROPE), F32)], 1)
    for m in range(3):
        tile = rope[32 * m : 32 * m + 16]
        if m < 2:
            tile = tile + pltpu.roll(rope[32 * m + 16 : 32 * m + 32], ROPE, 1)
        part[1, 32:48, 128 * m : 128 * m + 128] = tile
    part[1, 32:48, 384:512] = jnp.zeros((16, 128), F32)

    meet()
    cm.send("r1", part.at[1 - c], device(x, y, z, 1 - c), got1)
    cm.recv("r1", got1)
    mine[...] = part[c] + got1[...]
    cm.send("r2", mine, (seq, (1 - x_lo) * 2 + c), got2)
    cm.recv("r2", got2)
    full = mine[...] + got2[...]

    mean_square = jnp.sum(full * full, axis=1, keepdims=True) * (1.0 / LAT)
    normed = full * lax.rsqrt(mean_square + 1e-06) * gain_ref[...].astype(F32)
    cos_tiles, sin_tiles = [], []
    left = lanes((16, 128)) < 64
    for table, tiles in ((cos, cos_tiles), (sin, sin_tiles)):
        for m in range(2):
            tiles.append(
                jnp.where(left, table[32 * m : 32 * m + 16], table[32 * m + 16 : 32 * m + 32])
            )
        tiles += [table[64:80], jnp.zeros((16, 128), F32)]
    turned = rotated(
        full[32:48], jnp.concatenate(cos_tiles, 1), jnp.concatenate(sin_tiles, 1)
    )
    tail = jnp.where(c == 1, turned, normed[32:48])
    unit = jnp.concatenate([normed[0:32], tail], 0)
    unit = jnp.where(x_lo == 0, unit[:, 0:256], unit[:, 256:512]).astype(BF16)
    for g in range(2):
        KA[c, y, x, z, g] = unit[0:16, 128 * g : 128 * g + 128]
        KB[c, x, y, z, g] = unit[16:32, 128 * g : 128 * g + 128]
        KC[c, z, x, y, g] = unit[32:48, 128 * g : 128 * g + 128]
    gather_first(cm, KA, KB, KC)

    loads[2].wait()
    loads[3].wait()
    low = lanes((TOK, 128)) < 64
    for pair in range(HEADS // 2):
        t0, t1, t2 = (
            queries[:, 384 * pair + 128 * i : 384 * pair + 128 * i + 128] for i in range(3)
        )
        t1, t2 = t1.astype(F32), t2.astype(F32)
        second = pltpu.roll(jnp.where(low, t2, t1), 64, 1).astype(BF16)
        ropes = rotated(jnp.where(low, t1, t2), cos[...], sin[...]) * SCALE
        heads = []
        for i, nope in enumerate((t0, second)):
            head = 2 * pair + i
            lat = lax.dot_general(
                nope, wkey[:, 128 * head : 128 * head + 128], NT, preferred_element_type=F32
            )
            turned_q = jnp.where(low, pltpu.roll(ropes, 64, 1) if i else ropes, 0.0)
            heads.append(jnp.concatenate([lat * SCALE, turned_q], 1))
        for half in range(2):
            lo = half * HALF
            q[half * ROWS + TOK * pair : half * ROWS + TOK * pair + TOK] = jnp.concatenate(
                [heads[0][lo : lo + HALF], heads[1][lo : lo + HALF]], 0
            ).astype(BF16)
    top[...] = jnp.full_like(top, -1e30)
    total[...] = jnp.zeros_like(total)
    acc[...] = jnp.zeros_like(acc)

    gather_rest(cm, KA, KB, KC)

    def arrange(zz, carry):
        row0 = pl.multiple_of(zz * 320, 64)

        def put(row, cols, value):
            keys[pl.ds(pl.multiple_of(row, 16), value.shape[0]), cols] = value

        for yy in range(4):
            for xh in range(2):
                slot = yy * 2 + xh
                for g in range(4):
                    xx = 2 * xh + g // 2
                    cols = slice(128 * g, 128 * g + 128)
                    for core, base in ((0, 0), (1, EARLY)):
                        put(base + row0 + 16 * slot, cols, KA[core, yy, xx, zz, g % 2])
                        put(base + row0 + 128 + 16 * slot, cols, KB[core, xx, yy, zz, g % 2])
                cols = slice(512, 640)
                packed = [KC[1, zz, 2 * xh, yy, 0], KC[1, zz, 2 * xh, yy, 1]]
                swapped = [pltpu.roll(t.astype(F32), 64, 1).astype(BF16) for t in packed]
                put(row0 + 16 * slot, cols, packed[0])
                put(row0 + 128 + 16 * slot, cols, swapped[0])
                put(EARLY + row0 + 16 * slot, cols, swapped[1])
                put(EARLY + row0 + 128 + 16 * slot, cols, KC[1, zz, 2 * xh + 1, yy, 0])
        for yy in range(4):
            for g in range(5):
                cols = slice(128 * g, 128 * g + 128)
                if g < 4:
                    tiles = [KC[0, zz, 2 * xh + g // 2, yy, g % 2] for xh in range(2)]
                else:
                    tiles = [KC[1, zz, 2 * xh, yy, 1] for xh in range(2)]
                tiles = [t.astype(F32) for t in tiles]
                for base, lo in ((0, 0), (EARLY, 8)):
                    both = jnp.concatenate([t[lo : lo + 8] for t in tiles], 0).astype(BF16)
                    put(base + row0 + 256 + 16 * yy, cols, both)
        return carry

    lax.fori_loop(0, 8, arrange, 0)

    n_early = lax.div((z + 1) * 320 + STEP - 1, STEP)
    first_late = lax.div(z * 320, STEP)

    def offsets(i):
        j = i - 5
        late = 5 + jnp.minimum(first_late + j - n_early, 4)
        block = jnp.where(i < 5, i, jnp.where(j < n_early, j, late))
        rows = jnp.where((i < 5) | (j >= n_early), ROWS, 0)
        return pl.multiple_of(block * STEP, STEP), pl.multiple_of(rows, ROWS), j - n_early + first_late > 4

    def score(i, buffer):
        k0, q0, extra = offsets(i)
        s = lax.dot_general(
            q[pl.ds(q0, ROWS)], keys[pl.ds(k0, STEP)], NT, preferred_element_type=F32
        )
        limit = jnp.where(extra, -1, qpos[pl.ds(q0, ROWS)])
        allowed = kpos[0:1, pl.ds(k0, STEP)] <= jnp.concatenate([limit] * (STEP // 128), 1)
        scores[buffer] = jnp.where(allowed, s, -1e30)

    def absorb(i, buffer):
        k0, q0, _ = offsets(i)
        rows = pl.ds(q0, ROWS)
        s = scores[buffer]
        old = top[rows, 0:1]
        new = jnp.maximum(old, jnp.max(s, axis=1, keepdims=True))
        weights = jnp.exp(s - new)
        fade = jnp.exp(old - new)
        top[rows, 0:1] = new
        total[rows, 0:1] = total[rows, 0:1] * fade + jnp.sum(weights, axis=1, keepdims=True)
        product = jnp.dot(
            weights.astype(BF16), keys[pl.ds(k0, STEP), 0:LAT], preferred_element_type=F32
        )
        acc[rows] = acc[rows] * fade + product

    score(0, 0)

    def steps(n, carry):
        score(2 * n + 1, 1)
        absorb(2 * n, 0)
        score(jnp.minimum(2 * n + 2, 11), 0)
        absorb(2 * n + 1, 1)
        return carry

    lax.fori_loop(0, 6, steps, 0)

    loads[4].wait()
    for head in range(HEADS):
        halves = []
        for half in range(2):
            rows = slice(half * ROWS + head * HALF, half * ROWS + head * HALF + HALF)
            halves.append(acc[rows] / total[rows, 0:1])
        attended = jnp.concatenate(halves, 0).astype(BF16)
        cols = slice(128 * head, 128 * head + 128)
        out_ref[:, cols] = jnp.dot(
            attended, wvalue[:, cols], preferred_element_type=F32
        ).astype(BF16)
    cm.drain()


def on_device(hidden_in, w_down, kv_gain, queries, w_key, w_value):
    inverse = 10000.0 ** (-(np.arange(128) % 32) / 32.0)
    inverse = jnp.asarray(inverse.astype(np.float32)[None])
    vmem = pl.BlockSpec(memory_space=pltpu.VMEM)
    hbm = pl.BlockSpec(memory_space=pl.ANY)
    V = pltpu.VMEM
    return pl.pallas_call(
        body,
        out_shape=jax.ShapeDtypeStruct((TOK, HEADS * VDIM), BF16),
        in_specs=[hbm, hbm, vmem, vmem, hbm, hbm, hbm],
        out_specs=vmem,
        scratch_shapes=[
            V(hidden_in.shape, BF16),
            V(w_down.shape, BF16),
            V(queries.shape, BF16),
            V(w_key.shape, BF16),
            V(w_value.shape, BF16),
            V((2, 48, LAT), F32),
            V((48, LAT), F32),
            V((48, LAT), F32),
            V((48, LAT), F32),
            V((2, 4, 4, 8, 2, 16, 128), BF16),
            V((2, 4, 4, 8, 2, 16, 128), BF16),
            V((2, 8, 4, 4, 2, 16, 128), BF16),
            V((2 * EARLY, 640), BF16),
            V((2 * ROWS, 640), BF16),
            V((8, 2 * EARLY), jnp.int32),
            V((2 * ROWS, 128), jnp.int32),
            V((TOK, 128), F32),
            V((TOK, 128), F32),
            V((2, ROWS, STEP), F32),
            V((2 * ROWS, 128), F32),
            V((2 * ROWS, 128), F32),
            V((2 * ROWS, LAT), F32),
            pltpu.SemaphoreType.DMA((5,)),
            pltpu.SemaphoreType.DMA((N_SEMS,)),
            pltpu.SemaphoreType.DMA((N_SEMS,)),
        ],
        compiler_params=pltpu.CompilerParams(
            collective_id=0, has_side_effects=True, vmem_limit_bytes=56 * 2**20
        ),
        name="latent_attention",
    )(hidden_in, w_down, kv_gain.reshape(1, LAT), inverse, queries, w_key, w_value)


def solution(mesh):
    in_specs = (
        P("seq", "head"),
        P("head", None),
        P(),
        P("seq", "head"),
        P(None, "head"),
        P(None, "head"),
    )
    return jax.shard_map(
        on_device, mesh=mesh, in_specs=in_specs, out_specs=P("seq", "head"), check_vma=False
    )
```

time: 321 us -> 70.2 us (0.22)
  the two profiles are of different devices: /device:TPU:2 before, /device:TPU:1 now
where the time goes in v1:
time: 70.2 us; the launch traced here: 70 us
  Pallas kernels  62.9 us (90%)
  local copies, waits for them, and re-layouts  7.07 us (10%)
    pallas_call x1, Pallas kernels, on_device(): pl.pallas_call(body, out_shape=jax.ShapeDtypeStruct((TOK, HEADS * VDIM),...  62.9 us
    unnamed x2, local copies, waits for them, and re-layouts  5.81 us

profile of v1, /device:TPU:1, one launch (start us, length us, event | category | flops | bytes accessed | tf_op | source)
XLA Modules:
  0.0 70.0 jit_solution(15428433821173401994)
XLA Ops:
  0.0 1.3 %reshape.3.gain_ref = bf16[1,512]{1,0:T(2,128)(2,1)} reshape(bf16[512]{0:T(512)(128)(2,1)} %param.9) | data formatting | bytes 2048 | tf_op jit(solution)/shard_map/reshape | solution.py:479
  1.3 4.1 %copy.8.down_hbm = bf16[1792,576]{1,0:T(8,128)(2,1)} copy(bf16[1792,576]{0,1:T(8,128)(2,1)} %param.8) | data formatting | bytes 4128768 | tf_op args[1]
  5.4 62.9 %latent_attention.1 = bf16[80,2048]{1,0:T(8,128)(2,1)} custom-call(bf16[80,1792]{1,0:T(8,128)(2,1)} %hidden_hbm.1, bf16[1792,576]{1,0:T(8,128)(2,1)} %copy.8.down_hbm, bf16[1,512]{1,0:T(2,128)(2,1)} %reshape.3.gain_ref, f32[1,128]{1,0:T(1,128)} %constant.2.clone.inv_ref, bf16[80,3072]{1,0:T(8,128)(2,1)} %queries_hbm.1, bf16[512,2048]{1,0:T(8,128)(2,1)} %wkey_hbm.1, ...), custom_call_target="tpu_custom_call" | custom-call | tf_op jit(solution)/shard_map/latent_attention/pallas_call | solution.py:443
  68.3 1.7 %copy.10 = bf16[80,2048]{1,0:T(8,128)(2,1)} copy(bf16[80,2048]{1,0:T(8,128)(2,1)} %latent_attention.1) | data formatting | bytes 655360

commit v2 on v1

--- a/solution.py
+++ b/solution.py
@@ -79,19 +79,22 @@
     pl.semaphore_wait(pltpu.get_barrier_semaphore(), 7 + len(PLANE) + 1)
 
 
-def gather_first(cm, KA, KB, KC):
+def gather_first(cm, kind, ref):
     x, y, z, c = place()
+    if kind == "c":
+        order = sorted(PLANE, key=lambda t: -(min(t[0], 4 - t[0]) + min(t[1], 4 - t[1])))
+        for dx, dy in order:
+            cm.send(f"cp{dx}{dy}", ref.at[c, z, x, y], device(x + dx, y + dy, z, c))
+        return
+    unit = ref.at[c, y, x, z] if kind == "a" else ref.at[c, x, y, z]
     for dz in (4, 3, 5, 2, 6, 1, 7):
-        cm.send(f"az{dz}", KA.at[c, y, x, z], device(x, y, z + dz, c))
-        cm.send(f"bz{dz}", KB.at[c, x, y, z], device(x, y, z + dz, c))
-    order = sorted(PLANE, key=lambda t: -(min(t[0], 4 - t[0]) + min(t[1], 4 - t[1])))
-    for dx, dy in order:
-        cm.send(f"cp{dx}{dy}", KC.at[c, z, x, y], device(x + dx, y + dy, z, c))
-
-
-def gather_rest(cm, KA, KB, KC):
+        cm.send(f"{kind}z{dz}", unit, device(x, y, z + dz, c))
+
+
+def gather_rest(cm, KA, KB, KC, arrange_a, arrange_b, arrange_c):
     x, y, z, c = place()
     sibling = device(x, y, z, 1 - c)
+    other = 1 - c
 
     def X(d):
         return wrap(x + d, 4)
@@ -105,99 +108,122 @@
     def share(name, ref):
         cm.send("s" + name, ref, sibling)
 
-    for dz in range(1, 8):
-        cm.recv(f"az{dz}", KA.at[c, y, x, Z(-dz)])
-    for d in (1, -1):
-        cm.send(f"ax{d}", KA.at[c, y, x], device(x + d, y, z, c))
-    for d in (1, -1):
-        cm.send(f"ay{d}_0", KA.at[c, y, x], device(x, y + d, z, c))
-    cm.send("ax2", KA.at[c, y, x], device(x + 2, y, z, c))
-    share("a00", KA.at[c, y, x])
-    for dz in range(1, 8):
-        cm.recv(f"bz{dz}", KB.at[c, x, y, Z(-dz)])
-    for d in (1, -1):
-        cm.send(f"by{d}", KB.at[c, x, y], device(x, y + d, z, c))
-    for d in (1, -1):
-        cm.send(f"bx{d}_0", KB.at[c, x, y], device(x + d, y, z, c))
-    cm.send("by2", KB.at[c, x, y], device(x, y + 2, z, c))
-    share("b00", KB.at[c, x, y])
+    def col(kind, core, line, slot):
+        if kind == "a":
+            return KA.at[core, Y(line), X(slot)]
+        return KB.at[core, X(line), Y(slot)]
+
+    def across(kind, d):
+        return device(x + d, y, z, c) if kind == "a" else device(x, y + d, z, c)
+
+    def along(kind, d):
+        return device(x, y + d, z, c) if kind == "a" else device(x + d, y, z, c)
+
+    def start(kind):
+        for dz in range(1, 8):
+            unit = KA.at[c, y, x, Z(-dz)] if kind == "a" else KB.at[c, x, y, Z(-dz)]
+            cm.recv(f"{kind}z{dz}", unit)
+        own = col(kind, c, 0, 0)
+        for d in (1, -1):
+            cm.send(f"{kind}m{d}", own, across(kind, d))
+        cm.send(f"{kind}m2", own, across(kind, 2))
+        for d in (1, -1):
+            cm.send(f"{kind}l{d}_0", own, along(kind, d))
+        share(f"{kind}0_0", own)
+
+    def middle(kind, d):
+        cm.recv(f"{kind}m{d}", col(kind, c, 0, -d if d < 2 else 2))
+        slot = -d if d < 2 else 2
+        for e in (1, -1):
+            cm.send(f"{kind}l{e}_{slot}", col(kind, c, 0, slot), along(kind, e))
+        share(f"{kind}0_{slot}", col(kind, c, 0, slot))
+
+    def last(kind, e, slot):
+        cm.recv(f"{kind}l{e}_{slot}", col(kind, c, -e, slot))
+        if (e == 1) == (slot in (0, 1)):
+            cm.send(f"{kind}f_{slot}", col(kind, c, -e, slot), along(kind, e))
+        share(f"{kind}{-e}_{slot}", col(kind, c, -e, slot))
+
+    def far(kind, slot):
+        cm.recv(f"{kind}f_{slot}", col(kind, c, 2, slot))
+        share(f"{kind}2_{slot}", col(kind, c, 2, slot))
+
+    def ring(k, part):
+        rows = slice(2 * part, 2 * part + 2)
+        for d in (1, -1):
+            block = KC.at[c, Z(-d * k), rows]
+            if k > 0:
+                cm.recv(f"cz{d}_{k}_{part}", block)
+            if k < 3 or (d == 1) == (part == 0):
+                cm.send(f"cz{d}_{k + 1}_{part}", block, device(x, y, z + d, c))
+            if k > 0:
+                share(f"c{d * k}_{part}", block)
+
     for dx, dy in PLANE:
         cm.recv(f"cp{dx}{dy}", KC.at[c, z, X(-dx), Y(-dy)])
+    ring(0, 0)
+    ring(0, 1)
+    share("c0", KC.at[c, z])
+    start("a")
+    start("b")
+    ring(1, 0)
+    ring(1, 1)
     for d in (1, -1):
-        cm.send(f"cz{d}_1", KC.at[c, z], device(x, y, z + d, c))
-    share("c0", KC.at[c, z])
+        middle("a", d)
+        middle("b", d)
+    ring(2, 0)
+    last("a", 1, 0)
+    last("b", 1, 0)
+    middle("a", 2)
+    middle("b", 2)
+    ring(2, 1)
+    for e, slot in ((1, 1), (-1, -1)):
+        last("a", e, slot)
+        last("b", e, slot)
+    ring(3, 0)
+    for e, slot in ((-1, 2), (-1, 0)):
+        last("a", e, slot)
+        last("b", e, slot)
+    ring(3, 1)
+    for e, slot in ((1, -1), (-1, 1), (1, 2)):
+        last("a", e, slot)
+        last("b", e, slot)
+
+    def line_from_sibling(kind, d):
+        for slot in (0, 1, -1, 2):
+            cm.recv(f"s{kind}{d}_{slot}", col(kind, other, d, slot))
+
+    def planes_from_sibling(k):
+        for part in range(2):
+            cm.recv(f"sc{k}_{part}", KC.at[other, Z(-k), 2 * part : 2 * part + 2])
+
+    line_from_sibling("a", 0)
+    arrange_a(Y(0))
+    cm.recv("sc0", KC.at[other, z])
+    arrange_c(z)
+    for k in (1, -1, 2, -2):
+        planes_from_sibling(k)
+    lax.fori_loop(0, 4, lambda i, carry: (arrange_c(Z(jnp.where(i < 2, i - 2, i - 1))), carry)[1], 0)
     for d in (1, -1):
-        cm.recv(f"ax{d}", KA.at[c, y, X(-d)])
-        for e in (1, -1):
-            cm.send(f"ay{e}_{-d}", KA.at[c, y, X(-d)], device(x, y + e, z, c))
-        share(f"a0{-d}", KA.at[c, y, X(-d)])
-        cm.recv(f"by{d}", KB.at[c, x, Y(-d)])
-        for e in (1, -1):
-            cm.send(f"bx{e}_{-d}", KB.at[c, x, Y(-d)], device(x + e, y, z, c))
-        share(f"b0{-d}", KB.at[c, x, Y(-d)])
-
-    def pass_a(e, col):
-        cm.recv(f"ay{e}_{col}", KA.at[c, Y(-e), X(col)])
-        if (e == 1) == (col in (0, 1)):
-            cm.send(f"af_{col}", KA.at[c, Y(-e), X(col)], device(x, y + e, z, c))
-
-    def pass_b(e, col):
-        cm.recv(f"bx{e}_{col}", KB.at[c, X(-e), Y(col)])
-        if (e == 1) == (col in (0, 1)):
-            cm.send(f"bf_{col}", KB.at[c, X(-e), Y(col)], device(x + e, y, z, c))
-
-    def pass_c(k):
-        for d in (1, -1):
-            cm.recv(f"cz{d}_{k}", KC.at[c, Z(-d * k)])
-            if k < 3:
-                cm.send(f"cz{d}_{k + 1}", KC.at[c, Z(-d * k)], device(x, y, z + d, c))
-            else:
-                part = slice(0, 2) if d == 1 else slice(2, 4)
-                cm.send(f"cz{d}_4", KC.at[c, Z(-d * k), part], device(x, y, z + d, c))
-            share(f"cs{d}{k}", KC.at[c, Z(-d * k)])
-
-    pass_a(1, 0)
-    pass_b(1, 0)
-    pass_c(1)
-    cm.recv("ax2", KA.at[c, y, X(2)])
-    for e in (1, -1):
-        cm.send(f"ay{e}_2", KA.at[c, y, X(2)], device(x, y + e, z, c))
-    share("a02", KA.at[c, y, X(2)])
-    cm.recv("by2", KB.at[c, x, Y(2)])
-    for e in (1, -1):
-        cm.send(f"bx{e}_2", KB.at[c, x, Y(2)], device(x + e, y, z, c))
-    share("b02", KB.at[c, x, Y(2)])
-    for e, col in ((1, 1), (-1, -1)):
-        pass_a(e, col)
-        pass_b(e, col)
-    pass_c(2)
-    for e, col in ((-1, 2), (-1, 0), (1, -1), (-1, 1), (1, 2)):
-        pass_a(e, col)
-        pass_b(e, col)
-    for d in (1, -1):
-        share(f"a{d}", KA.at[c, Y(d)])
-        share(f"b{d}", KB.at[c, X(d)])
-    pass_c(3)
-    for col in (0, 1, -1, 2):
-        cm.recv(f"af_{col}", KA.at[c, Y(2), X(col)])
-        cm.recv(f"bf_{col}", KB.at[c, X(2), Y(col)])
-    share("a2", KA.at[c, Y(2)])
-    share("b2", KB.at[c, X(2)])
-    cm.recv("cz1_4", KC.at[c, Z(4), 0:2])
-    cm.recv("cz-1_4", KC.at[c, Z(4), 2:4])
-    share("c4", KC.at[c, Z(4)])
-    o = 1 - c
-    for d in (0, 1, -1, 2):
-        cm.recv(f"sa0{d}", KA.at[o, y, X(d)])
-        cm.recv(f"sb0{d}", KB.at[o, x, Y(d)])
-    for d in (1, -1, 2):
-        cm.recv(f"sa{d}", KA.at[o, Y(d)])
-        cm.recv(f"sb{d}", KB.at[o, X(d)])
-    cm.recv("sc0", KC.at[o, z])
-    for k in (1, 2, 3):
-        for d in (1, -1):
-            cm.recv(f"scs{d}{k}", KC.at[o, Z(-d * k)])
-    cm.recv("sc4", KC.at[o, Z(4)])
+        line_from_sibling("a", d)
+        arrange_a(Y(d))
+    for part in range(2):
+        block = KC.at[c, Z(4), 2 * part : 2 * part + 2]
+        cm.recv(f"cz{1 if part == 0 else -1}_4_{part}", block)
+        share(f"c4_{part}", block)
+    for slot in (0, 1, -1, 2):
+        far("a", slot)
+        far("b", slot)
+    for d in (0, 1, -1):
+        line_from_sibling("b", d)
+    arrange_b(x >> 1)
+    for k in (3, -3, 4):
+        planes_from_sibling(k)
+    lax.fori_loop(0, 3, lambda i, carry: (arrange_c(Z(i + 3)), carry)[1], 0)
+    line_from_sibling("a", 2)
+    arrange_a(Y(2))
+    line_from_sibling("b", 2)
+    arrange_b(1 - (x >> 1))
 
 
 def lanes(shape):
@@ -236,7 +262,7 @@
             )
         )
     ]
-    for load in loads:
+    for load in loads[:2]:
         load.start()
     greet()
     cm = Comm(send_sems, recv_sems)
@@ -268,7 +294,9 @@
 
     loads[0].wait()
     loads[1].wait()
-    partial = jnp.dot(hidden[...], down[...], preferred_element_type=F32)
+    for load in loads[2:]:
+        load.start()
+    partial = lax.dot_general(hidden[...], down[...], NT, preferred_element_type=F32)
     part[0] = partial[0:48, 0:LAT]
     part[1, 0:32] = partial[48:80, 0:LAT]
     rope = jnp.concatenate([partial[:, LAT:], jnp.zeros((TOK, 128 - ROPE), F32)], 1)
@@ -280,34 +308,43 @@
     part[1, 32:48, 384:512] = jnp.zeros((16, 128), F32)
 
     meet()
-    cm.send("r1", part.at[1 - c], device(x, y, z, 1 - c), got1)
-    cm.recv("r1", got1)
-    mine[...] = part[c] + got1[...]
-    cm.send("r2", mine, (seq, (1 - x_lo) * 2 + c), got2)
-    cm.recv("r2", got2)
-    full = mine[...] + got2[...]
-
-    mean_square = jnp.sum(full * full, axis=1, keepdims=True) * (1.0 / LAT)
-    normed = full * lax.rsqrt(mean_square + 1e-06) * gain_ref[...].astype(F32)
+    tiles = [slice(16 * t, 16 * t + 16) for t in range(3)]
+    order = (2, 0, 1)
+    for t in order:
+        cm.send(f"r1_{t}", part.at[1 - c, tiles[t]], device(x, y, z, 1 - c), got1.at[tiles[t]])
+    for t in order:
+        cm.recv(f"r1_{t}", got1.at[tiles[t]])
+        mine[tiles[t]] = part[c, tiles[t]] + got1[tiles[t]]
+        cm.send(
+            f"r2_{t}", mine.at[tiles[t]], (seq, (1 - x_lo) * 2 + c), got2.at[tiles[t]]
+        )
+    gain = gain_ref[...].astype(F32).reshape(1, LAT)
     cos_tiles, sin_tiles = [], []
     left = lanes((16, 128)) < 64
-    for table, tiles in ((cos, cos_tiles), (sin, sin_tiles)):
+    for table, picked in ((cos, cos_tiles), (sin, sin_tiles)):
         for m in range(2):
-            tiles.append(
+            picked.append(
                 jnp.where(left, table[32 * m : 32 * m + 16], table[32 * m + 16 : 32 * m + 32])
             )
-        tiles += [table[64:80], jnp.zeros((16, 128), F32)]
-    turned = rotated(
-        full[32:48], jnp.concatenate(cos_tiles, 1), jnp.concatenate(sin_tiles, 1)
-    )
-    tail = jnp.where(c == 1, turned, normed[32:48])
-    unit = jnp.concatenate([normed[0:32], tail], 0)
-    unit = jnp.where(x_lo == 0, unit[:, 0:256], unit[:, 256:512]).astype(BF16)
-    for g in range(2):
-        KA[c, y, x, z, g] = unit[0:16, 128 * g : 128 * g + 128]
-        KB[c, x, y, z, g] = unit[16:32, 128 * g : 128 * g + 128]
-        KC[c, z, x, y, g] = unit[32:48, 128 * g : 128 * g + 128]
-    gather_first(cm, KA, KB, KC)
+        picked += [table[64:80], jnp.zeros((16, 128), F32)]
+    cos_keys, sin_keys = jnp.concatenate(cos_tiles, 1), jnp.concatenate(sin_tiles, 1)
+    for t in order:
+        cm.recv(f"r2_{t}", got2.at[tiles[t]])
+        full = mine[tiles[t]] + got2[tiles[t]]
+        mean_square = jnp.sum(full * full, axis=1, keepdims=True) * (1.0 / LAT)
+        unit = full * lax.rsqrt(mean_square + 1e-06) * gain
+        if t == 2:
+            unit = jnp.where(c == 1, rotated(full, cos_keys, sin_keys), unit)
+        unit = jnp.where(x_lo == 0, unit[:, 0:256], unit[:, 256:512]).astype(BF16)
+        for g in range(2):
+            tile = unit[:, 128 * g : 128 * g + 128]
+            if t == 0:
+                KA[c, y, x, z, g] = tile
+            elif t == 1:
+                KB[c, x, y, z, g] = tile
+            else:
+                KC[c, z, x, y, g] = tile
+        gather_first(cm, "abc"[t], (KA, KB, KC)[t])
 
     loads[2].wait()
     loads[3].wait()
@@ -336,25 +373,41 @@
     total[...] = jnp.zeros_like(total)
     acc[...] = jnp.zeros_like(acc)
 
-    gather_rest(cm, KA, KB, KC)
-
-    def arrange(zz, carry):
-        row0 = pl.multiple_of(zz * 320, 64)
-
-        def put(row, cols, value):
-            keys[pl.ds(pl.multiple_of(row, 16), value.shape[0]), cols] = value
-
+
+    def put(row, cols, value):
+        keys[pl.ds(pl.multiple_of(row, 16), value.shape[0]), cols] = value
+
+    def arrange_a(yy):
+        def one(zz, carry):
+            for xh in range(2):
+                for g in range(4):
+                    cols = slice(128 * g, 128 * g + 128)
+                    for core in range(2):
+                        row = core * EARLY + zz * 320 + 16 * (yy * 2 + xh)
+                        put(row, cols, KA[core, yy, 2 * xh + g // 2, zz, g % 2])
+            return carry
+
+        lax.fori_loop(0, 8, one, 0)
+
+    def arrange_b(xh):
+        def one(zz, carry):
+            for yy in range(4):
+                for g in range(4):
+                    cols = slice(128 * g, 128 * g + 128)
+                    for core in range(2):
+                        row = core * EARLY + zz * 320 + 128 + 16 * (yy * 2 + xh)
+                        put(row, cols, KB[core, 2 * xh + g // 2, yy, zz, g % 2])
+            return carry
+
+        lax.fori_loop(0, 8, one, 0)
+
+    def arrange_c(zz):
+        row0 = zz * 320
         for yy in range(4):
             for xh in range(2):
                 slot = yy * 2 + xh
-                for g in range(4):
-                    xx = 2 * xh + g // 2
-                    cols = slice(128 * g, 128 * g + 128)
-                    for core, base in ((0, 0), (1, EARLY)):
-                        put(base + row0 + 16 * slot, cols, KA[core, yy, xx, zz, g % 2])
-                        put(base + row0 + 128 + 16 * slot, cols, KB[core, xx, yy, zz, g % 2])
                 cols = slice(512, 640)
-                packed = [KC[1, zz, 2 * xh, yy, 0], KC[1, zz, 2 * xh, yy, 1]]
+                packed = [KC[1, zz, 2 * xh, yy, g] for g in range(2)]
                 swapped = [pltpu.roll(t.astype(F32), 64, 1).astype(BF16) for t in packed]
                 put(row0 + 16 * slot, cols, packed[0])
                 put(row0 + 128 + 16 * slot, cols, swapped[0])
@@ -364,16 +417,15 @@
             for g in range(5):
                 cols = slice(128 * g, 128 * g + 128)
                 if g < 4:
-                    tiles = [KC[0, zz, 2 * xh + g // 2, yy, g % 2] for xh in range(2)]
+                    both = [KC[0, zz, 2 * xh + g // 2, yy, g % 2] for xh in range(2)]
                 else:
-                    tiles = [KC[1, zz, 2 * xh, yy, 1] for xh in range(2)]
-                tiles = [t.astype(F32) for t in tiles]
+                    both = [KC[1, zz, 2 * xh, yy, 1] for xh in range(2)]
+                both = [t.astype(F32) for t in both]
                 for base, lo in ((0, 0), (EARLY, 8)):
-                    both = jnp.concatenate([t[lo : lo + 8] for t in tiles], 0).astype(BF16)
-                    put(base + row0 + 256 + 16 * yy, cols, both)
-        return carry
-
-    lax.fori_loop(0, 8, arrange, 0)
+                    rows = jnp.concatenate([t[lo : lo + 8] for t in both], 0).astype(BF16)
+                    put(base + row0 + 256 + 16 * yy, cols, rows)
+
+    gather_rest(cm, KA, KB, KC, arrange_a, arrange_b, arrange_c)
 
     n_early = lax.div((z + 1) * 320 + STEP - 1, STEP)
     first_late = lax.div(z * 320, STEP)
@@ -398,24 +450,26 @@
         k0, q0, _ = offsets(i)
         rows = pl.ds(q0, ROWS)
         s = scores[buffer]
-        old = top[rows, 0:1]
+        old = top[rows]
         new = jnp.maximum(old, jnp.max(s, axis=1, keepdims=True))
-        weights = jnp.exp(s - new)
+        weights = jnp.exp(s - jnp.concatenate([new] * (STEP // 128), 1))
         fade = jnp.exp(old - new)
-        top[rows, 0:1] = new
-        total[rows, 0:1] = total[rows, 0:1] * fade + jnp.sum(weights, axis=1, keepdims=True)
+        top[rows] = new
+        total[rows] = total[rows] * fade + (
+            (weights[:, 0:128] + weights[:, 128:256]) + (weights[:, 256:384] + weights[:, 384:512])
+        )
         product = jnp.dot(
             weights.astype(BF16), keys[pl.ds(k0, STEP), 0:LAT], preferred_element_type=F32
         )
-        acc[rows] = acc[rows] * fade + product
+        acc[rows] = acc[rows] * jnp.concatenate([fade] * (LAT // 128), 1) + product
 
     score(0, 0)
 
     def steps(n, carry):
+        absorb(2 * n, 0)
         score(2 * n + 1, 1)
-        absorb(2 * n, 0)
+        absorb(2 * n + 1, 1)
         score(jnp.minimum(2 * n + 2, 11), 0)
-        absorb(2 * n + 1, 1)
         return carry
 
     lax.fori_loop(0, 6, steps, 0)
@@ -425,7 +479,7 @@
         halves = []
         for half in range(2):
             rows = slice(half * ROWS + head * HALF, half * ROWS + head * HALF + HALF)
-            halves.append(acc[rows] / total[rows, 0:1])
+            halves.append(acc[rows] / jnp.sum(total[rows], axis=1, keepdims=True))
         attended = jnp.concatenate(halves, 0).astype(BF16)
         cols = slice(128 * head, 128 * head + 128)
         out_ref[:, cols] = jnp.dot(
@@ -447,7 +501,7 @@
         out_specs=vmem,
         scratch_shapes=[
             V(hidden_in.shape, BF16),
-            V(w_down.shape, BF16),
+            V(w_down.shape[::-1], BF16),
             V(queries.shape, BF16),
             V(w_key.shape, BF16),
             V(w_value.shape, BF16),
@@ -476,7 +530,7 @@
             collective_id=0, has_side_effects=True, vmem_limit_bytes=56 * 2**20
         ),
         name="latent_attention",
-    )(hidden_in, w_down, kv_gain.reshape(1, LAT), inverse, queries, w_key, w_value)
+    )(hidden_in, w_down.T, kv_gain, inverse, queries, w_key, w_value)
 
 
 def solution(mesh):

time: 70.2 us -> 59 us (0.84)
  Pallas kernels: 62.9 us -> 57.1 us
  local copies, waits for them, and re-layouts: 7.07 us -> 1.72 us
    pallas_call x1, Pallas kernels: 62.9 us -> 57.1 us  [on_device(): pl.pallas_call(body, out_shape=jax.ShapeDtypeStruct((TOK, HEADS * VDIM),...]
    unnamed x2 -> x1, local copies, waits for them, and re-layouts: 5.81 us -> 1.72 us
    reshape x1 -> x0, local copies, waits for them, and re-layouts: 1.26 us -> none  [on_device(): kv_gain.reshape(1, LAT)]
where the time goes in v2:
time: 59 us; the launch traced here: 58.9 us
  Pallas kernels  57.1 us (97%)
  local copies, waits for them, and re-layouts  1.72 us (3%)
    pallas_call x1, Pallas kernels, on_device(): pl.pallas_call(body, out_shape=jax.ShapeDtypeStruct((TOK, HEADS * VDIM),...  57.1 us
    unnamed x1, local copies, waits for them, and re-layouts  1.72 us

profile of v2, /device:TPU:1, one launch (start us, length us, event | category | flops | bytes accessed | tf_op | source)
XLA Modules:
  0.0 58.9 jit_solution(11256374164886149649)
XLA Ops:
  0.0 57.1 %latent_attention.1 = bf16[80,2048]{1,0:T(8,128)(2,1)} custom-call(bf16[80,1792]{1,0:T(8,128)(2,1)} %hidden_hbm.1, bf16[576,1792]{1,0:T(8,128)(2,1)} %bitcast.1, bf16[512]{0:T(512)(128)(2,1)} %gain_ref.1, f32[1,128]{1,0:T(1,128)} %constant.2.clone.inv_ref, bf16[80,3072]{1,0:T(8,128)(2,1)} %queries_hbm.1, bf16[512,2048]{1,0:T(8,128)(2,1)} %wkey_hbm.1, ...), custom_call_target="tpu_custom_call" | custom-call | tf_op jit(solution)/shard_map/latent_attention/pallas_call | solution.py:497
  57.2 1.7 %copy.9 = bf16[80,2048]{1,0:T(8,128)(2,1)} copy(bf16[80,2048]{1,0:T(8,128)(2,1)} %latent_attention.1) | data formatting | bytes 655360

commit v3 on v2

--- a/solution.py
+++ b/solution.py
@@ -15,26 +15,26 @@
 TOK, HALF, HEADS = 80, 40, 16
 ROWS = HALF * HEADS
 EARLY = 2560
-STEP = 512
+STEP = 1280
+DEEP = 896
 NT = (((1,), (1,)), ((), ()))
 SCALE = (NOPE + ROPE) ** (-0.5)
 N_SEMS = 160
 
 
 def wrap(value, size):
-    return lax.rem(value + 2 * size, size)
+    return value & (size - 1)
 
 
 def place():
     s = lax.axis_index("seq")
     h = lax.axis_index("head")
-    x = lax.rem(lax.div(s, 4), 2) * 2 + lax.div(h, 2)
-    return x, lax.rem(s, 4), lax.div(s, 8), lax.rem(h, 2)
+    return ((s >> 2) & 1) * 2 + (h >> 1), s & 3, s >> 3, h & 1
 
 
 def device(x, y, z, c):
     x, y, z = wrap(x, 4), wrap(y, 4), wrap(z, 8)
-    return (z * 8 + lax.div(x, 2) * 4 + y, lax.rem(x, 2) * 2 + c)
+    return (z * 8 + (x >> 1) * 4 + y, (x & 1) * 2 + c)
 
 
 class Comm:
@@ -168,26 +168,32 @@
     start("b")
     ring(1, 0)
     ring(1, 1)
-    for d in (1, -1):
-        middle("a", d)
-        middle("b", d)
+    for kind in "ab":
+        middle(kind, 1)
+    for kind in "ab":
+        middle(kind, -1)
     ring(2, 0)
-    last("a", 1, 0)
-    last("b", 1, 0)
-    middle("a", 2)
-    middle("b", 2)
     ring(2, 1)
-    for e, slot in ((1, 1), (-1, -1)):
-        last("a", e, slot)
-        last("b", e, slot)
+    for kind in "ab":
+        last(kind, 1, 0)
+    for kind in "ab":
+        middle(kind, 2)
+    for kind in "ab":
+        last(kind, 1, 1)
+    for kind in "ab":
+        last(kind, -1, -1)
     ring(3, 0)
-    for e, slot in ((-1, 2), (-1, 0)):
-        last("a", e, slot)
-        last("b", e, slot)
     ring(3, 1)
-    for e, slot in ((1, -1), (-1, 1), (1, 2)):
-        last("a", e, slot)
-        last("b", e, slot)
+    for kind in "ab":
+        last(kind, -1, 2)
+    for kind in "ab":
+        last(kind, -1, 0)
+    for kind in "ab":
+        last(kind, 1, -1)
+    for kind in "ab":
+        last(kind, -1, 1)
+    for kind in "ab":
+        last(kind, 1, 2)
 
     def line_from_sibling(kind, d):
         for slot in (0, 1, -1, 2):
@@ -242,27 +248,28 @@
 
 
 def body(
-    hidden_hbm, down_hbm, gain_ref, inv_ref, queries_hbm, wkey_hbm, wvalue_hbm, out_ref,
-    hidden, down, queries, wkey, wvalue, part, got1, mine, got2, KA, KB, KC,
+    hidden_hbm, down_hbm, gain_ref, inv_ref, queries_hbm, wkey_hbm, wvalue_hbm, out_hbm,
+    hidden, down, queries, wkey, wvalue, result, part, got1, mine, got2, KA, KB, KC,
     keys, q, kpos, qpos, cos, sin, scores, top, total, acc,
     load_sems, send_sems, recv_sems,
 ):
     x, y, z, c = place()
     seq = lax.axis_index("seq")
-    x_lo = lax.rem(x, 2)
+    x_lo = x & 1
     loads = [
         pltpu.make_async_copy(src, dst, load_sems.at[i])
         for i, (src, dst) in enumerate(
             (
                 (hidden_hbm, hidden),
-                (down_hbm, down),
+                (down_hbm.at[:, 0:DEEP], down.at[:, 0:DEEP]),
+                (down_hbm.at[:, DEEP:], down.at[:, DEEP:]),
                 (queries_hbm, queries),
                 (wkey_hbm, wkey),
                 (wvalue_hbm, wvalue),
             )
         )
     ]
-    for load in loads[:2]:
+    for load in loads[:3]:
         load.start()
     greet()
     cm = Comm(send_sems, recv_sems)
@@ -294,9 +301,15 @@
 
     loads[0].wait()
     loads[1].wait()
-    for load in loads[2:]:
+    for load in loads[3:]:
         load.start()
-    partial = lax.dot_general(hidden[...], down[...], NT, preferred_element_type=F32)
+    partial = lax.dot_general(
+        hidden[:, 0:DEEP], down[:, 0:DEEP], NT, preferred_element_type=F32
+    )
+    loads[2].wait()
+    partial = partial + lax.dot_general(
+        hidden[:, DEEP:], down[:, DEEP:], NT, preferred_element_type=F32
+    )
     part[0] = partial[0:48, 0:LAT]
     part[1, 0:32] = partial[48:80, 0:LAT]
     rope = jnp.concatenate([partial[:, LAT:], jnp.zeros((TOK, 128 - ROPE), F32)], 1)
@@ -346,8 +359,8 @@
                 KC[c, z, x, y, g] = tile
         gather_first(cm, "abc"[t], (KA, KB, KC)[t])
 
-    loads[2].wait()
     loads[3].wait()
+    loads[4].wait()
     low = lanes((TOK, 128)) < 64
     for pair in range(HEADS // 2):
         t0, t1, t2 = (
@@ -427,27 +440,25 @@
 
     gather_rest(cm, KA, KB, KC, arrange_a, arrange_b, arrange_c)
 
-    n_early = lax.div((z + 1) * 320 + STEP - 1, STEP)
-    first_late = lax.div(z * 320, STEP)
+    upper = z >= 4
 
     def offsets(i):
-        j = i - 5
-        late = 5 + jnp.minimum(first_late + j - n_early, 4)
-        block = jnp.where(i < 5, i, jnp.where(j < n_early, j, late))
-        rows = jnp.where((i < 5) | (j >= n_early), ROWS, 0)
-        return pl.multiple_of(block * STEP, STEP), pl.multiple_of(rows, ROWS), j - n_early + first_late > 4
+        fourth = jnp.where(upper, 1, 2)
+        block = jnp.where(i < 2, i, jnp.where(i == 2, 0, jnp.where(i == 3, fourth, 3)))
+        rows = jnp.where((i == 2) | ((i == 3) & upper), 0, ROWS)
+        return pl.multiple_of(block * STEP, STEP), pl.multiple_of(rows, ROWS)
 
     def score(i, buffer):
-        k0, q0, extra = offsets(i)
+        k0, q0 = offsets(i)
         s = lax.dot_general(
             q[pl.ds(q0, ROWS)], keys[pl.ds(k0, STEP)], NT, preferred_element_type=F32
         )
-        limit = jnp.where(extra, -1, qpos[pl.ds(q0, ROWS)])
+        limit = qpos[pl.ds(q0, ROWS)]
         allowed = kpos[0:1, pl.ds(k0, STEP)] <= jnp.concatenate([limit] * (STEP // 128), 1)
         scores[buffer] = jnp.where(allowed, s, -1e30)
 
     def absorb(i, buffer):
-        k0, q0, _ = offsets(i)
+        k0, q0 = offsets(i)
         rows = pl.ds(q0, ROWS)
         s = scores[buffer]
         old = top[rows]
@@ -456,7 +467,7 @@
         fade = jnp.exp(old - new)
         top[rows] = new
         total[rows] = total[rows] * fade + (
-            (weights[:, 0:128] + weights[:, 128:256]) + (weights[:, 256:384] + weights[:, 384:512])
+            sum(weights[:, i : i + 128] for i in range(0, STEP, 128))
         )
         product = jnp.dot(
             weights.astype(BF16), keys[pl.ds(k0, STEP), 0:LAT], preferred_element_type=F32
@@ -469,23 +480,35 @@
         absorb(2 * n, 0)
         score(2 * n + 1, 1)
         absorb(2 * n + 1, 1)
-        score(jnp.minimum(2 * n + 2, 11), 0)
+        score(2 * n + 2, 0)
         return carry
 
-    lax.fori_loop(0, 6, steps, 0)
-
-    loads[4].wait()
+    lax.fori_loop(0, 2, steps, 0)
+    absorb(4, 0)
+
+    loads[5].wait()
+    leaving = []
     for head in range(HEADS):
         halves = []
         for half in range(2):
             rows = slice(half * ROWS + head * HALF, half * ROWS + head * HALF + HALF)
-            halves.append(acc[rows] / jnp.sum(total[rows], axis=1, keepdims=True))
+            halves.append(acc[rows] * (1.0 / jnp.sum(total[rows], axis=1, keepdims=True)))
         attended = jnp.concatenate(halves, 0).astype(BF16)
         cols = slice(128 * head, 128 * head + 128)
-        out_ref[:, cols] = jnp.dot(
+        result[:, cols] = jnp.dot(
             attended, wvalue[:, cols], preferred_element_type=F32
         ).astype(BF16)
+        if head % 4 == 3:
+            cols = slice(128 * head - 384, 128 * head + 128)
+            leaving.append(
+                pltpu.make_async_copy(
+                    result.at[:, cols], out_hbm.at[:, cols], load_sems.at[6 + head // 4]
+                )
+            )
+            leaving[-1].start()
     cm.drain()
+    for copy in leaving:
+        copy.wait()
 
 
 def on_device(hidden_in, w_down, kv_gain, queries, w_key, w_value):
@@ -498,13 +521,14 @@
         body,
         out_shape=jax.ShapeDtypeStruct((TOK, HEADS * VDIM), BF16),
         in_specs=[hbm, hbm, vmem, vmem, hbm, hbm, hbm],
-        out_specs=vmem,
+        out_specs=hbm,
         scratch_shapes=[
             V(hidden_in.shape, BF16),
             V(w_down.shape[::-1], BF16),
             V(queries.shape, BF16),
             V(w_key.shape, BF16),
             V(w_value.shape, BF16),
+            V((TOK, HEADS * VDIM), BF16),
             V((2, 48, LAT), F32),
             V((48, LAT), F32),
             V((48, LAT), F32),
@@ -522,7 +546,7 @@
             V((2 * ROWS, 128), F32),
             V((2 * ROWS, 128), F32),
             V((2 * ROWS, LAT), F32),
-            pltpu.SemaphoreType.DMA((5,)),
+            pltpu.SemaphoreType.DMA((10,)),
             pltpu.SemaphoreType.DMA((N_SEMS,)),
             pltpu.SemaphoreType.DMA((N_SEMS,)),
         ],

time: 59 us -> 58.4 us (0.990)
  Pallas kernels: 57.1 us -> 56.5 us
    pallas_call x1, Pallas kernels: 57.1 us -> 56.5 us  [on_device(): pl.pallas_call(body, out_shape=jax.ShapeDtypeStruct((TOK, HEADS * VDIM),...]
where the time goes in v3:
time: 58.4 us; the launch traced here: 58.3 us
  Pallas kernels  56.5 us (97%)
  local copies, waits for them, and re-layouts  1.72 us (3%)
    pallas_call x1, Pallas kernels, on_device(): pl.pallas_call(body, out_shape=jax.ShapeDtypeStruct((TOK, HEADS * VDIM),...  56.5 us
    unnamed x1, local copies, waits for them, and re-layouts  1.72 us

profile of v3, /device:TPU:1, one launch (start us, length us, event | category | flops | bytes accessed | tf_op | source)
XLA Modules:
  0.0 58.3 jit_solution(16526901082729890390)
XLA Ops:
  0.0 56.5 %latent_attention.1 = bf16[80,2048]{1,0:T(8,128)(2,1)} custom-call(bf16[80,1792]{1,0:T(8,128)(2,1)} %hidden_hbm.1, bf16[576,1792]{1,0:T(8,128)(2,1)} %bitcast.1, bf16[512]{0:T(512)(128)(2,1)} %gain_ref.1, f32[1,128]{1,0:T(1,128)} %constant.2.clone.inv_ref, bf16[80,3072]{1,0:T(8,128)(2,1)} %queries_hbm.1, bf16[512,2048]{1,0:T(8,128)(2,1)} %wkey_hbm.1, ...), custom_call_target="tpu_custom_call" | custom-call | tf_op jit(solution)/shard_map/latent_attention/pallas_call | solution.py:520
  56.6 1.7 %copy.9 = bf16[80,2048]{1,0:T(8,128)(2,1)} copy(bf16[80,2048]{1,0:T(8,128)(2,1)} %latent_attention.1) | data formatting | bytes 655360

commit v4 on v3

--- a/solution.py
+++ b/solution.py
@@ -249,7 +249,7 @@
 
 def body(
     hidden_hbm, down_hbm, gain_ref, inv_ref, queries_hbm, wkey_hbm, wvalue_hbm, out_hbm,
-    hidden, down, queries, wkey, wvalue, result, part, got1, mine, got2, KA, KB, KC,
+    hidden, down, queries, wkey, wvalue, result, part, got1, mine, got2, norm_out, norm_in, KA, KB, KC,
     keys, q, kpos, qpos, cos, sin, scores, top, total, acc,
     load_sems, send_sems, recv_sems,
 ):
@@ -327,11 +327,15 @@
         cm.send(f"r1_{t}", part.at[1 - c, tiles[t]], device(x, y, z, 1 - c), got1.at[tiles[t]])
     for t in order:
         cm.recv(f"r1_{t}", got1.at[tiles[t]])
-        mine[tiles[t]] = part[c, tiles[t]] + got1[tiles[t]]
-        cm.send(
-            f"r2_{t}", mine.at[tiles[t]], (seq, (1 - x_lo) * 2 + c), got2.at[tiles[t]]
-        )
+        both = part[c, tiles[t]] + got1[tiles[t]]
+        mine[0, tiles[t]] = both[:, 0:256]
+        mine[1, tiles[t]] = both[:, 256:512]
+        norm_out[tiles[t]] = mine[x_lo, tiles[t]].astype(BF16)
+        partner = (seq, (1 - x_lo) * 2 + c)
+        cm.send(f"r2_{t}", mine.at[1 - x_lo, tiles[t]], partner, got2.at[tiles[t]])
+        cm.send(f"r3_{t}", norm_out.at[tiles[t]], partner, norm_in.at[tiles[t]])
     gain = gain_ref[...].astype(F32).reshape(1, LAT)
+    gain = jnp.where(x_lo == 0, gain[:, 0:256], gain[:, 256:512])
     cos_tiles, sin_tiles = [], []
     left = lanes((16, 128)) < 64
     for table, picked in ((cos, cos_tiles), (sin, sin_tiles)):
@@ -340,15 +344,20 @@
                 jnp.where(left, table[32 * m : 32 * m + 16], table[32 * m + 16 : 32 * m + 32])
             )
         picked += [table[64:80], jnp.zeros((16, 128), F32)]
-    cos_keys, sin_keys = jnp.concatenate(cos_tiles, 1), jnp.concatenate(sin_tiles, 1)
+    cos_keys, sin_keys = (
+        jnp.concatenate([jnp.where(x_lo == 0, p[i], p[i + 2]) for i in range(2)], 1)
+        for p in (cos_tiles, sin_tiles)
+    )
     for t in order:
         cm.recv(f"r2_{t}", got2.at[tiles[t]])
-        full = mine[tiles[t]] + got2[tiles[t]]
-        mean_square = jnp.sum(full * full, axis=1, keepdims=True) * (1.0 / LAT)
+        cm.recv(f"r3_{t}", norm_in.at[tiles[t]])
+        full = mine[x_lo, tiles[t]] + got2[tiles[t]]
+        rest = mine[1 - x_lo, tiles[t]] + norm_in[tiles[t]].astype(F32)
+        mean_square = jnp.sum(full * full + rest * rest, axis=1, keepdims=True) * (1.0 / LAT)
         unit = full * lax.rsqrt(mean_square + 1e-06) * gain
         if t == 2:
             unit = jnp.where(c == 1, rotated(full, cos_keys, sin_keys), unit)
-        unit = jnp.where(x_lo == 0, unit[:, 0:256], unit[:, 256:512]).astype(BF16)
+        unit = unit.astype(BF16)
         for g in range(2):
             tile = unit[:, 128 * g : 128 * g + 128]
             if t == 0:
@@ -531,8 +540,10 @@
             V((TOK, HEADS * VDIM), BF16),
             V((2, 48, LAT), F32),
             V((48, LAT), F32),
-            V((48, LAT), F32),
-            V((48, LAT), F32),
+            V((2, 48, 256), F32),
+            V((48, 256), F32),
+            V((48, 256), BF16),
+            V((48, 256), BF16),
             V((2, 4, 4, 8, 2, 16, 128), BF16),
             V((2, 4, 4, 8, 2, 16, 128), BF16),
             V((2, 8, 4, 4, 2, 16, 128), BF16),

time: 58.4 us -> 57.9 us (level)
  no operation moved by 1% of the time
where the time goes in v4:
time: 57.9 us; the launch traced here: 57.7 us
  Pallas kernels  56 us (97%)
  local copies, waits for them, and re-layouts  1.72 us (3%)
    pallas_call x1, Pallas kernels, on_device(): pl.pallas_call(body, out_shape=jax.ShapeDtypeStruct((TOK, HEADS * VDIM),...  56 us
    unnamed x1, local copies, waits for them, and re-layouts  1.72 us

profile of v4, /device:TPU:1, one launch (start us, length us, event | category | flops | bytes accessed | tf_op | source)
XLA Modules:
  0.0 57.7 jit_solution(6154997310550041704)
XLA Ops:
  0.0 56.0 %latent_attention.1 = bf16[80,2048]{1,0:T(8,128)(2,1)} custom-call(bf16[80,1792]{1,0:T(8,128)(2,1)} %hidden_hbm.1, bf16[576,1792]{1,0:T(8,128)(2,1)} %bitcast.1, bf16[512]{0:T(512)(128)(2,1)} %gain_ref.1, f32[1,128]{1,0:T(1,128)} %constant.2.clone.inv_ref, bf16[80,3072]{1,0:T(8,128)(2,1)} %queries_hbm.1, bf16[512,2048]{1,0:T(8,128)(2,1)} %wkey_hbm.1, ...), custom_call_target="tpu_custom_call" | custom-call | tf_op jit(solution)/shard_map/latent_attention/pallas_call | solution.py:529
  56.0 1.7 %copy.9 = bf16[80,2048]{1,0:T(8,128)(2,1)} copy(bf16[80,2048]{1,0:T(8,128)(2,1)} %latent_attention.1) | data formatting | bytes 655360

commit v5 on v4

--- a/solution.py
+++ b/solution.py
@@ -323,10 +323,9 @@
     meet()
     tiles = [slice(16 * t, 16 * t + 16) for t in range(3)]
     order = (2, 0, 1)
+    cm.send("r1", part.at[1 - c], device(x, y, z, 1 - c), got1)
+    cm.recv("r1", got1)
     for t in order:
-        cm.send(f"r1_{t}", part.at[1 - c, tiles[t]], device(x, y, z, 1 - c), got1.at[tiles[t]])
-    for t in order:
-        cm.recv(f"r1_{t}", got1.at[tiles[t]])
         both = part[c, tiles[t]] + got1[tiles[t]]
         mine[0, tiles[t]] = both[:, 0:256]
         mine[1, tiles[t]] = both[:, 256:512]

time: 57.9 us -> 58 us (level)
  no operation moved by 1% of the time
where the time goes in v5:
time: 58 us; the launch traced here: 57.8 us
  Pallas kernels  56.1 us (97%)
  local copies, waits for them, and re-layouts  1.72 us (3%)
    pallas_call x1, Pallas kernels, on_device(): pl.pallas_call(body, out_shape=jax.ShapeDtypeStruct((TOK, HEADS * VDIM),...  56.1 us
    unnamed x1, local copies, waits for them, and re-layouts  1.72 us

profile of v5, /device:TPU:1, one launch (start us, length us, event | category | flops | bytes accessed | tf_op | source)
XLA Modules:
  0.0 57.8 jit_solution(1741081348392373807)
XLA Ops:
  0.0 56.1 %latent_attention.1 = bf16[80,2048]{1,0:T(8,128)(2,1)} custom-call(bf16[80,1792]{1,0:T(8,128)(2,1)} %hidden_hbm.1, bf16[576,1792]{1,0:T(8,128)(2,1)} %bitcast.1, bf16[512]{0:T(512)(128)(2,1)} %gain_ref.1, f32[1,128]{1,0:T(1,128)} %constant.2.clone.inv_ref, bf16[80,3072]{1,0:T(8,128)(2,1)} %queries_hbm.1, bf16[512,2048]{1,0:T(8,128)(2,1)} %wkey_hbm.1, ...), custom_call_target="tpu_custom_call" | custom-call | tf_op jit(solution)/shard_map/latent_attention/pallas_call | solution.py:528
  56.1 1.7 %copy.9 = bf16[80,2048]{1,0:T(8,128)(2,1)} copy(bf16[80,2048]{1,0:T(8,128)(2,1)} %latent_attention.1) | data formatting | bytes 655360
